TPU v7x, 512 devices: a whole 4x8x8 slice. The times are simulated.
512 devices in a mesh: fsdp: 64 (over z, y), tensor: 8 (over x, core).
Axes of the slice: x: 4, y: 8, z: 8, core: 2. Of those that a mesh axis runs over, the one named last changes fastest.
Arguments:
- momentum: bfloat16 [16384, 30720], P('fsdp', 'tensor'), may hold values from -12.5 to 12.5
- right_prev: bfloat16 [30720, 256], P(('tensor', 'fsdp')), may hold values from -4 to 4
Outputs:
- new_momentum: bfloat16 [16384, 30720], P('fsdp', 'tensor')
- left_factor: float32 [16384, 256], P('fsdp')
- right_factor: bfloat16 [30720, 256], P(('tensor', 'fsdp'))
All inputs are finite; a program needn't handle non-finite values.
Results may differ from a plain program's by a relative error of at most 0.004.
Values may be sent and summed in bfloat16 or wider, within the bound.
A program may use at most 64 MiB of HBM per device.

v0:
```python
import math

import jax
import jax.numpy as jnp
from jax import lax
from jax.sharding import PartitionSpec as P

D = 16384
FF = 30720


def gram_matrix(block_rows):
    return lax.dot_general(
        block_rows,
        block_rows,
        (((0,), (0,)), ((), ())),
        precision=lax.Precision.HIGHEST,
        preferred_element_type=jnp.float32,
    )


def whiten(block_rows, summed_gram):
    cholesky_factor = jnp.linalg.cholesky(summed_gram)
    return lax.linalg.triangular_solve(
        cholesky_factor, block_rows, left_side=False, lower=True, transpose_a=True
    )


def body(momentum, right_prev):
    columns = momentum
    partial_value = jnp.dot(
        columns,
        lax.all_gather(right_prev, "fsdp", axis=0, tiled=True),
        preferred_element_type=jnp.float32,
    )
    left_raw = lax.psum(partial_value, "tensor")
    first_gram = lax.psum(gram_matrix(left_raw), "fsdp")
    left = whiten(left_raw, first_gram)
    left_factor = math.sqrt(D) * left
    left_low = left.astype(jnp.bfloat16)
    columns = momentum
    right_share = lax.psum_scatter(
        lax.dot_general(
            columns, left_low, (((0,), (0,)), ((), ())), preferred_element_type=jnp.float32
        ),
        "fsdp",
        scatter_dimension=0,
        tiled=True,
    )
    squares = lax.psum(jnp.sum(right_share * right_share, axis=0), ("fsdp", "tensor"))
    columns = momentum
    update = lax.dot_general(
        left_low,
        lax.all_gather(right_share.astype(jnp.bfloat16), "fsdp", axis=0, tiled=True),
        (((1,), (1,)), ((), ())),
        preferred_element_type=jnp.float32,
    )
    new_momentum = (columns.astype(jnp.float32) - 0.5 * update).astype(jnp.bfloat16)
    column_scale = lax.rsqrt(squares / FF + 1e-06)
    right_factor = (right_share * column_scale[None, :]).astype(jnp.bfloat16)
    return (new_momentum, left_factor, right_factor)


def solution(mesh):
    in_specs = (P("fsdp", "tensor"), P(("tensor", "fsdp"), None))
    out_specs = (P("fsdp", "tensor"), P("fsdp", None), P(("tensor", "fsdp"), None))
    return jax.shard_map(body, mesh=mesh, in_specs=in_specs, out_specs=out_specs, check_vma=False)
```

profile of v0, /device:TPU:1, one launch (start us, length us, event | category | flops | bytes accessed | tf_op | source)
XLA Modules:
  0.0 676.5 jit_solution(10790632436804818551)
XLA Ops:
  8.0 88.4 %all-gather.5.cloned.1.call-done = bf16[64,60,256]{2,1,0:T(8,128)(2,1)} async-done(((bf16[1,60,256]{2,1,0:T(8,128)(2,1)}), bf16[64,60,256]{2,1,0:T(8,128)(2,1)}) %all-gather.5.cloned.1.call-update) | async-done | bytes 1966096 | tf_op jit(solution)/shard_map/all_gather | solution.py:33
  96.4 3.8 reshape.44
  100.2 2.9 fusion.18
  103.2 69.9 %all-reduce.6.cloned.1.call-done = f32[256,256]{1,0:T(8,128)} async-done(((f32[256,256]{1,0:T(8,128)}), f32[256,256]{1,0:T(8,128)}) %all-reduce.6.cloned.1.call-update) | async-done | bytes 262160 | tf_op jit(solution)/shard_map/psum | solution.py:36
  173.0 2.3 fusion.19
  175.5 150.2 %all-reduce.8.cloned.1.call-done = f32[256,256]{0,1:T(8,128)} async-done(((f32[256,256]{0,1:T(8,128)}), f32[256,256]{0,1:T(8,128)}) %all-reduce.8.cloned.1.call-update) | async-done | bytes 262160 | tf_op jit(solution)/shard_map/psum | solution.py:37
  325.6 1.1 copy.15
  326.7 1.0 fusion.2
  327.7 11.7 %cholesky.50 = f32[128,128]{1,0:T(8,128)S(1)} custom-call(f32[128,128]{1,0:T(8,128)S(1)} %cholesky.118), custom_call_target="Cholesky" | custom-call | tf_op jit(solution)/shard_map/jit(cholesky)/cholesky | solution.py:23
  339.5 9.8 %custom-call.14 = f32[1,128,128]{1,2,0:T(8,128)S(1)} custom-call(f32[1,128,128]{2,1,0:T(8,128)S(1)} %get-tuple-element.33), custom_call_target="InvertDiagBlocksLowerTriangular" | custom-call | tf_op jit(solution)/shard_map/jit(cholesky)/cholesky | solution.py:23
  349.8 11.7 %cholesky.105 = f32[128,128]{1,0:T(8,128)S(1)} custom-call(f32[128,128]{1,0:T(8,128)S(1)} %convolution_subtract_fusion.1), custom_call_target="Cholesky" | custom-call | tf_op jit(solution)/shard_map/jit(cholesky)/cholesky | solution.py:23
  363.6 4.1 while.1
  364.3 1.4 bitcast_dynamic-update-slice_fusion.2
  366.3 1.4 bitcast_dynamic-update-slice_fusion.2
  367.7 19.7 %custom-call.15 = f32[2,128,128]{1,2,0:T(8,128)S(1)} custom-call(f32[2,128,128]{2,1,0:T(8,128)S(1)} %get-tuple-element.10), custom_call_target="InvertDiagBlocksLowerTriangular" | custom-call | tf_op jit(solution)/shard_map/triangular_solve | solution.py:24
  388.5 2.6 convolution_bitcast_fusion
  391.1 1.3 dynamic-slice.3
  393.0 164.6 %all-reduce.10.cloned.1.call-done = f32[3840,256]{0,1:T(8,128)} async-done(((f32[3840,256]{0,1:T(8,128)}), f32[3840,256]{0,1:T(8,128)}) %all-reduce.10.cloned.1.call-update) | async-done | bytes 3932176
  557.6 1.0 fusion.7
  560.2 1.1 multiply_reduce_fusion
  561.4 99.5 %psum.23 = f32[256]{0:T(256)S(1)} all-reduce(f32[256]{0:T(256)S(1)} %multiply_reduce_fusion), channel_id=1, replica_groups=mesh['fsdp'=64,'tensor'=8] {'fsdp','tensor'}, use_global_device_ids=true, to_apply=%region_8.9 | all-reduce | flops 256 | bytes 2048 | tf_op jit(solution)/shard_map/psum | solution.py:50
  660.9 1.1 multiply_convert_fusion
  662.7 3.7 reshape.46
  666.4 3.5 fusion.1
  (38 shorter events, 6.8 us)
Async XLA Ops:
  7.2 89.2 %all-gather.5.cloned.1.call-start = ((), (), s32[]{:S(2)}) async-start(), calls=%async_computation.2 | async-start | bytes 2129920 | tf_op jit(solution)/shard_map/all_gather | solution.py:33
  7.9 92.3 %copy-start = (bf16[256,3840]{1,0:T(8,128)(2,1)S(1)}, bf16[256,3840]{1,0:T(8,128)(2,1)}, u32[]{:S(2)}) copy-start(bf16[256,3840]{1,0:T(8,128)(2,1)} %param.2) | copy-start | bytes 5898244
  7.9 165.1 %all-reduce.6.cloned.1.call-start = ((), (), s32[]{:S(2)}) async-start(), calls=%async_computation | async-start | bytes 524288 | tf_op jit(solution)/shard_map/psum | solution.py:36
  103.1 222.5 %all-reduce.8.cloned.1.call-start = ((), (), s32[]{:S(2)}) async-start(), calls=%async_computation.1 | async-start | bytes 524288 | tf_op jit(solution)/shard_map/psum | solution.py:37
  175.4 382.2 %all-reduce.10.cloned.1.call-start = ((), (), s32[]{:S(2)}) async-start(), calls=%async_computation.4 | async-start | bytes 7864320
  175.4 212.0 %copy-start.1 = (f32[256,256]{1,0:T(8,128)S(1)}, f32[256,256]{1,0:T(8,128)}, u32[]{:S(2)}) copy-start(f32[256,256]{1,0:T(8,128)} %all-reduce.6.cloned.1.call-done) | copy-start | bytes 786436
  391.1 271.6 %all-gather.7.cloned.1.call-start = ((), (), s32[]{:S(2)}) async-start(), calls=%async_computation.3 | async-start | bytes 2129920 | tf_op jit(solution)/shard_map/all_gather | solution.py:54
Sparse Core Ops, SparseCore 0:
  11.1 85.2 all-gather.4
  103.2 69.7 all-reduce.5
  177.1 148.4 all-reduce.7
  391.2 166.3 all-reduce.9
  561.1 79.9 all-gather.6
where the time goes:
time: 677 us; the launch traced here: 676 us
  waiting for transfers between devices  474 us (70%)
  blocking collectives  99.5 us (15%)
  other arithmetic  56.9 us (8%)
  local copies, waits for them, and re-layouts  17.2 us (3%)
  between operations  15.9 us (2%)
  matrix products  12.9 us (2%)
    unnamed x6, waiting for transfers between devices  165 us
    psum x1, waiting for transfers between devices, body(): first_gram = lax.psum(gram_matrix(left_raw), 'fsdp')  150 us
    psum x1, blocking collectives, body(): lax.psum(jnp.sum(right_share * right_share, axis=0), ('fsdp', 'tensor'))  99.5 us
    all_gather x1, waiting for transfers between devices, body(): lax.all_gather(right_prev, 'fsdp', axis=0, tiled=True)  88.4 us
    psum x1, waiting for transfers between devices, body(): left_raw = lax.psum(partial_value, 'tensor')  69.9 us
    another operation x6, other arithmetic, whiten(): cholesky_factor = jnp.linalg.cholesky(summed_gram)  34 us
    another operation x3, other arithmetic, whiten(): lax.linalg.triangular_solve(cholesky_factor, block_rows, left_side=False,...  19.7 us
  transfers between devices with their start and end apart: 5, of which 4 were waited for; matrix products, arithmetic and copies ran while one was open for 1% of the time, Pallas kernels for 0%

commit v1 on v0

v1 whole, which is shorter than its diff:
```python
import math

import jax
import jax.numpy as jnp
from jax import lax
from jax.experimental import pallas as pl
from jax.experimental.pallas import tpu as pltpu
from jax.sharding import PartitionSpec as P

D = 16384
FF = 30720
RANK = 256
ROWS = 256
COLS = 3840
SHARE = 60
PAD = 64
N = 8
HALF = 128
MESH = pl.DeviceIdType.MESH
F32 = jnp.float32
BF16 = jnp.bfloat16
HIGHEST = lax.Precision.HIGHEST
VMEM_LIMIT = 56 * 1024 * 1024


def place():
    f, t = lax.axis_index("fsdp"), lax.axis_index("tensor")
    return lax.div(f, N), lax.rem(f, N), t


def up(i, d):
    return lax.rem(i + d, N)


def remote(src, dst, send, recv, z, y, t):
    return pltpu.make_async_remote_copy(
        src_ref=src,
        dst_ref=dst,
        send_sem=send,
        recv_sem=recv,
        device_id=(z * N + y, t),
        device_id_type=MESH,
    )


def greet(z, y, t):
    barrier = pltpu.get_barrier_semaphore()
    for d in range(1, N):
        for there in ((z, up(y, d), t), (up(z, d), y, t), (z, y, up(t, d))):
            pl.semaphore_signal(
                barrier, inc=1, device_id=(there[0] * N + there[1], there[2]), device_id_type=MESH
            )
    pl.semaphore_wait(barrier, 3 * (N - 1))


def exchange(axis, here, src_of, dst_of, send, recv):
    z, y, t = here
    me = here[axis]
    sent, waits = [], []
    for d in (4, 3, 5, 2, 6, 1, 7):
        peer = up(me, d)
        there = [z, y, t]
        there[axis] = peer
        copy = remote(src_of(peer), dst_of(me), send.at[d], recv.at[d], *there)
        copy.start()
        sent.append(copy)
        origin = up(me, N - d)
        waits.append(remote(src_of(peer), dst_of(origin), send.at[d], recv.at[d], *there))
    return sent, waits


def gather_first(here, buf, send, recv):
    z, y, _ = here
    one, one_waits = exchange(
        1, here, lambda p: buf.at[0, z, y], lambda i: buf.at[0, z, i], send.at[0], recv.at[0]
    )
    two, two_waits = exchange(
        0, here, lambda p: buf.at[1, z, y], lambda i: buf.at[1, i, y], send.at[1], recv.at[1]
    )
    return one + two, one_waits + two_waits


def strip(buf, half, i, unit):
    if half == 0:
        return buf.at[0, i, pl.ds(4 * unit, 4)]
    return buf.at[1, pl.ds(4 * unit, 4), i]


def ring_peer(here, half, way):
    z, y, t = here
    step = 1 if way == 0 else N - 1
    return (up(z, step), y, t) if half == 0 else (z, up(y, step), t)


STREAMS = [(unit, half, way) for unit in (0, 1) for half in (0, 1) for way in (0, 1)]


def gather_second(here, buf, send, recv):
    sent = []

    def arrived(half, way, s, unit):
        me = here[half]
        i = up(me, N - 1 - s) if way == 0 else up(me, 1 + s)
        dst = strip(buf, half, i, unit)
        remote(
            dst, dst, send.at[half, way, s, unit], recv.at[half, way, s, unit],
            *ring_peer(here, half, way),
        ).wait_recv()

    for s in range(4):
        for unit, half, way in STREAMS:
            if s == 3 and unit != way:
                continue
            if s > 0:
                arrived(half, way, s - 1, unit)
            me = here[half]
            i = up(me, N - s) if way == 0 else up(me, s)
            src = strip(buf, half, i, unit)
            copy = remote(
                src, src, send.at[half, way, s, unit], recv.at[half, way, s, unit],
                *ring_peer(here, half, way),
            )
            copy.start()
            sent.append(copy)
    for unit, half, way in STREAMS:
        if unit != way:
            arrived(half, way, 2, unit)
    for unit, half, way in STREAMS:
        if unit == way:
            arrived(half, way, 3, unit)
    return sent


def spread(offset, transposed):
    shape = (HALF, 256) if transposed else (256, HALF)
    n = lax.broadcasted_iota(jnp.int32, shape, 0 if transposed else 1)
    k = lax.broadcasted_iota(jnp.int32, shape, 1 if transposed else 0)
    high = n >= PAD
    want = offset + n - jnp.where(high, PAD - SHARE, 0)
    inside = n - jnp.where(high, PAD, 0) < SHARE
    return jnp.where((k == want) & inside, 1.0, 0.0).astype(BF16)


def first_kernel(
    m_ref, r_ref, left_ref, gram_ref, wide_ref,
    buf, mpad, part, got, gram, tile_y, tile_z,
    a_send, a_recv, b_send, b_recv, c_send, c_recv,
):
    here = place()
    z, y, t = here
    n = lax.broadcasted_iota(jnp.int32, (PAD, SHARE), 0)
    k = lax.broadcasted_iota(jnp.int32, (PAD, SHARE), 1)
    longer = jnp.where(n == k, 1.0, 0.0).astype(BF16)
    for half in (0, 1):
        buf[half, z, y] = jnp.dot(
            longer, r_ref[:, half * HALF:(half + 1) * HALF], preferred_element_type=F32
        ).astype(BF16)
    greet(z, y, t)
    sent, waits = gather_first(here, buf, a_send, a_recv)

    for i in range(COLS // 120):
        start = min(120 * i // 128 * 128, COLS - 256)
        window = m_ref[:, start:start + 256]
        mpad[:, i * 128:(i + 1) * 128] = jnp.dot(
            window, spread(120 * i - start, False), preferred_element_type=F32
        ).astype(BF16)
        wide_ref[i * 128:(i + 1) * 128, :] = lax.dot_general(
            spread(120 * i - start, True), window, (((1,), (1,)), ((), ())),
            preferred_element_type=F32,
        ).astype(BF16)

    for copy in waits:
        copy.wait_recv()
    sent += gather_second(here, buf, b_send, b_recv)

    width = N * PAD
    for half in (0, 1):
        total = jnp.zeros((ROWS, HALF), F32)
        for i in range(N):
            total += jnp.dot(
                mpad[:, i * width:(i + 1) * width],
                buf[half, i].reshape(width, HALF),
                preferred_element_type=F32,
            )
        part[:, half * HALF:(half + 1) * HALF] = total

    rows = ROWS // N
    piece = lambda i: pl.ds(pl.multiple_of(i * rows, rows), rows)
    more, waits = exchange(
        2, here, lambda p: part.at[piece(p)], lambda i: got.at[i], c_send.at[0], c_recv.at[0]
    )
    sent += more
    got[t] = part[piece(t), :]
    for copy in waits:
        copy.wait_recv()
    own = got[0]
    for i in range(1, N):
        own += got[i]
    left_ref[piece(t), :] = own
    more, waits = exchange(
        2, here, lambda p: left_ref.at[piece(t)], lambda i: left_ref.at[piece(i)],
        c_send.at[1], c_recv.at[1],
    )
    sent += more
    for copy in waits:
        copy.wait_recv()

    rows_all = left_ref[...]
    product = lax.dot_general(
        rows_all, rows_all, (((0,), (0,)), ((), ())),
        precision=HIGHEST, preferred_element_type=F32,
    )
    for i in range(64):
        r, c = i // 2 * 8, i % 2 * 128
        gram[i] = product[r:r + 8, c:c + 128]
    more, waits = exchange(
        1, here, lambda p: gram.at[t * N + p], lambda i: tile_y.at[i], c_send.at[2], c_recv.at[2]
    )
    sent += more
    tile_y[y] = gram[t * N + y]
    for copy in waits:
        copy.wait_recv()
    total = tile_y[0]
    for i in range(1, N):
        total += tile_y[i]
    tile_z[z] = total
    more, waits = exchange(
        0, here, lambda p: tile_z.at[z], lambda i: tile_z.at[i], c_send.at[3], c_recv.at[3]
    )
    sent += more
    for copy in waits:
        copy.wait_recv()
    total = tile_z[0]
    for i in range(1, N):
        total += tile_z[i]
    gram_ref[t * N + y] = total
    more, waits = exchange(
        1, here, lambda p: gram_ref.at[t * N + y], lambda i: gram_ref.at[t * N + i],
        c_send.at[4], c_recv.at[4],
    )
    sent += more
    for copy in waits:
        copy.wait_recv()
    block = lambda i: gram_ref.at[pl.ds(pl.multiple_of(i * N, N), N)]
    more, waits = exchange(
        2, here, lambda p: block(t), lambda i: block(i), c_send.at[5], c_recv.at[5]
    )
    sent += more
    for copy in waits:
        copy.wait_recv()
    for copy in sent:
        copy.wait_send()


def first(momentum, right_prev):
    dma = pltpu.SemaphoreType.DMA
    return pl.pallas_call(
        first_kernel,
        out_shape=(
            jax.ShapeDtypeStruct((ROWS, RANK), F32),
            jax.ShapeDtypeStruct((64, 8, 128), F32),
            jax.ShapeDtypeStruct((64 * PAD, ROWS), BF16),
        ),
        in_specs=[pl.BlockSpec(memory_space=pltpu.VMEM)] * 2,
        out_specs=[pl.BlockSpec(memory_space=pltpu.VMEM)] * 3,
        scratch_shapes=[
            pltpu.VMEM((2, N, N, PAD, HALF), BF16),
            pltpu.VMEM((ROWS, 64 * PAD), BF16),
            pltpu.VMEM((ROWS, RANK), F32),
            pltpu.VMEM((N, ROWS // N, RANK), F32),
            pltpu.VMEM((64, 8, 128), F32),
            pltpu.VMEM((N, 8, 128), F32),
            pltpu.VMEM((N, 8, 128), F32),
            dma((2, N)), dma((2, N)),
            dma((2, 2, 4, 2)), dma((2, 2, 4, 2)),
            dma((6, N)), dma((6, N)),
        ],
        compiler_params=pltpu.CompilerParams(
            collective_id=0, has_side_effects=True, vmem_limit_bytes=VMEM_LIMIT
        ),
    )(momentum, right_prev)


def invert_cholesky(w):
    lane = lax.broadcasted_iota(jnp.int32, (8, 128), 1)
    sub = lax.broadcasted_iota(jnp.int32, (8, 128), 0)
    row_of = lambda v, k: jnp.broadcast_to(v[k:k + 1, :], (8, 128))
    depth = 32
    for p in range(RANK // depth):
        base = p * depth
        b0 = base // 128
        rows = [
            [w[base + 8 * a:base + 8 * a + 8, 128 * b:128 * b + 128] for b in (0, 1)]
            for a in range(depth // 8)
        ]
        for q in range(depth // 8):
            l0 = (base + 8 * q) % 128
            below = range(q, depth // 8)
            cols = {
                a: [
                    jnp.broadcast_to(rows[a][b0][:, l0 + k:l0 + k + 1], (8, 128))
                    for k in range(8)
                ]
                for a in below
            }
            for k in range(8):
                inv = lax.rsqrt(row_of(cols[q][k], k))
                here = lane == l0 + k
                fresh = [row_of(rows[q][b], k) for b in (0, 1)]
                fresh[b0] = jnp.where(here, 1.0, fresh[b0])
                fresh = [v * inv for v in fresh]
                scaled = {k2: row_of(cols[q][k2], k) * inv for k2 in range(k + 1, 8)}
                for a in below:
                    mult = cols[a][k] * inv
                    if a == q:
                        mult = jnp.where(sub > k, mult, 0.0)
                    for b in (0, 1):
                        old = rows[a][b]
                        if b == b0:
                            erase = here & (sub > k) if a == q else here
                            old = jnp.where(erase, 0.0, old)
                        new = old - mult * fresh[b]
                        if a == q:
                            new = jnp.where(sub == k, fresh[b], new)
                        rows[a][b] = new
                    for k2 in range(k + 1, 8):
                        cols[a][k2] = cols[a][k2] - mult * scaled[k2]
        panel = jnp.concatenate([jnp.concatenate(r, axis=1) for r in rows], axis=0)
        w[base:base + depth, :] = panel
        end = base + depth
        if end < RANK:
            first_row = end // 128 * 128
            at = lax.broadcasted_iota(jnp.int32, (depth, RANK), 1) - base
            over = (at > lax.broadcasted_iota(jnp.int32, (depth, RANK), 0)) & (at < depth)
            update = lax.dot_general(
                panel[:, first_row:], jnp.where(over, 0.0, panel), (((0,), (0,)), ((), ())),
                precision=HIGHEST, preferred_element_type=F32,
            )[end - first_row:, :]
            col = lax.broadcasted_iota(jnp.int32, (RANK - end, RANK), 1)
            old = jnp.where((col >= base) & (col < end), 0.0, w[end:, :])
            w[end:, :] = old - update


def whiten_kernel(left_ref, gram_ref, factor_ref, low_ref, w):
    for i in range(64):
        r, c = i // 2 * 8, i % 2 * 128
        w[r:r + 8, c:c + 128] = gram_ref[i]
    invert_cholesky(w)
    row = lax.broadcasted_iota(jnp.int32, (RANK, RANK), 0)
    col = lax.broadcasted_iota(jnp.int32, (RANK, RANK), 1)
    inverse = jnp.where(col <= row, w[...], 0.0)
    left = lax.dot_general(
        left_ref[...], inverse, (((1,), (1,)), ((), ())),
        precision=HIGHEST, preferred_element_type=F32,
    )
    factor_ref[...] = math.sqrt(D) * left
    low_ref[...] = left.astype(BF16)


def whiten(left_raw, gram):
    return pl.pallas_call(
        whiten_kernel,
        out_shape=(
            jax.ShapeDtypeStruct((ROWS, RANK), F32),
            jax.ShapeDtypeStruct((ROWS, RANK), BF16),
        ),
        in_specs=[pl.BlockSpec(memory_space=pltpu.VMEM)] * 2,
        out_specs=[pl.BlockSpec(memory_space=pltpu.VMEM)] * 2,
        scratch_shapes=[pltpu.VMEM((RANK, RANK), F32)],
        compiler_params=pltpu.CompilerParams(vmem_limit_bytes=VMEM_LIMIT),
    )(left_raw, gram)


def last_kernel(
    m_ref, wide_ref, low_ref, new_ref, right_ref,
    part, away, land, near, rest, buf, packed, sq_y, sq_z, sq_t,
    a_send, a_recv, b_send, b_recv, r_send, r_recv, d_send, d_recv, s_send, s_recv,
):
    here = place()
    z, y, t = here
    low = low_ref[...]
    width = N * PAD
    for i in range(N):
        product = jnp.dot(
            wide_ref[i * width:(i + 1) * width, :], low, preferred_element_type=F32
        )
        for half in (0, 1):
            part[half, i] = product[:, half * HALF:(half + 1) * HALF].reshape(N, PAD, HALF)
    greet(z, y, t)
    sent = []

    def arrived(half, way, s, unit):
        dst = land.at[half, way, s, unit]
        remote(
            dst, dst, r_send.at[half, way, s, unit], r_recv.at[half, way, s, unit],
            *ring_peer(here, half, way),
        ).wait_recv()

    for s in range(4):
        for unit, half, way in STREAMS:
            if s == 0 and unit != way:
                continue
            me = here[half]
            dest = up(me, 4 - s) if way == 0 else up(me, 4 + s)
            own = strip(part, half, dest, unit)[...]
            if s == 0 or (s == 1 and unit != way):
                src = away.at[half, way, unit]
                src[...] = own.astype(BF16)
            else:
                arrived(half, way, s - 1, unit)
                src = land.at[half, way, s - 1, unit]
                src[...] = (src[...].astype(F32) + own).astype(BF16)
            copy = remote(
                src, land.at[half, way, s, unit],
                r_send.at[half, way, s, unit], r_recv.at[half, way, s, unit],
                *ring_peer(here, half, way),
            )
            copy.start()
            sent.append(copy)
    for half in (0, 1):
        for unit in (0, 1):
            for way in (0, 1):
                arrived(half, way, 3, unit)
            mine = strip(part, half, here[half], unit)
            near[half, pl.ds(4 * unit, 4)] = (
                mine[...]
                + land[half, 0, 3, unit].astype(F32)
                + land[half, 1, 3, unit].astype(F32)
            )
    share = []
    for half in (0, 1):
        more, waits = exchange(
            1 - half, here, lambda p: near.at[half, p], lambda i: rest.at[half, i],
            d_send.at[half], d_recv.at[half],
        )
        sent += more
        rest[half, here[1 - half]] = near[half, here[1 - half]]
        share.append(waits)
    for half in (0, 1):
        for copy in share[half]:
            copy.wait_recv()
        total = rest[half, 0]
        for i in range(1, N):
            total += rest[half, i]
        share[half] = total
        buf[half, z, y] = total.astype(BF16)

    more, gather_waits = gather_first(here, buf, a_send, a_recv)
    sent += more
    squares = [jnp.sum(v * v, axis=0, keepdims=True) for v in share]
    sq_y[y] = jnp.concatenate(squares + [jnp.zeros((6, HALF), F32)], axis=0)
    total = None
    for axis, tiles, after in ((1, sq_y, sq_z), (0, sq_z, sq_t)):
        me = here[axis]
        more, waits = exchange(
            axis, here, lambda p: tiles.at[me], lambda i: tiles.at[i],
            s_send.at[axis], s_recv.at[axis],
        )
        sent += more
        if axis == 0:
            for copy in gather_waits:
                copy.wait_recv()
        for copy in waits:
            copy.wait_recv()
        total = tiles[0]
        for i in range(1, N):
            total += tiles[i]
        after[here[0] if axis == 1 else t] = total
    more, square_waits = exchange(
        2, here, lambda p: sq_t.at[t], lambda i: sq_t.at[i], s_send.at[2], s_recv.at[2]
    )
    sent += more
    sent += gather_second(here, buf, b_send, b_recv)

    group = 4 * SHARE
    n = lax.broadcasted_iota(jnp.int32, (group, 256), 0)
    k = lax.broadcasted_iota(jnp.int32, (group, 256), 1)
    skip = sum(jnp.where(n >= SHARE * i, PAD - SHARE, 0) for i in (1, 2, 3))
    close = jnp.where(k == n + skip, 1.0, 0.0).astype(BF16)
    for g in range(16):
        for half in (0, 1):
            wide = buf[half, g // 2, g % 2 * 4:g % 2 * 4 + 4].reshape(256, HALF)
            packed[g * group:(g + 1) * group, half * HALF:(half + 1) * HALF] = jnp.dot(
                close, wide, preferred_element_type=F32
            ).astype(BF16)
    step = 768
    for i in range(COLS // step):
        update = lax.dot_general(
            low, packed[i * step:(i + 1) * step, :], (((1,), (1,)), ((), ())),
            preferred_element_type=F32,
        )
        block = m_ref[:, i * step:(i + 1) * step].astype(F32)
        new_ref[:, i * step:(i + 1) * step] = (block - 0.5 * update).astype(BF16)

    for copy in square_waits:
        copy.wait_recv()
    total = sq_t[0]
    for i in range(1, N):
        total += sq_t[i]
    scale = lax.rsqrt(total / FF + 1e-06)
    right = jnp.concatenate([share[0] * scale[0:1, :], share[1] * scale[1:2, :]], axis=1)
    right_ref[...] = right[:SHARE, :].astype(BF16)
    for copy in sent:
        copy.wait_send()


def last(momentum, wide, low):
    dma = pltpu.SemaphoreType.DMA
    return pl.pallas_call(
        last_kernel,
        out_shape=(
            jax.ShapeDtypeStruct((ROWS, COLS), BF16),
            jax.ShapeDtypeStruct((SHARE, RANK), BF16),
        ),
        in_specs=[pl.BlockSpec(memory_space=pltpu.VMEM)] * 3,
        out_specs=[pl.BlockSpec(memory_space=pltpu.VMEM)] * 2,
        scratch_shapes=[
            pltpu.VMEM((2, N, N, PAD, HALF), F32),
            pltpu.VMEM((2, 2, 2, 4, PAD, HALF), BF16),
            pltpu.VMEM((2, 2, 4, 2, 4, PAD, HALF), BF16),
            pltpu.VMEM((2, N, PAD, HALF), F32),
            pltpu.VMEM((2, N, PAD, HALF), F32),
            pltpu.VMEM((2, N, N, PAD, HALF), BF16),
            pltpu.VMEM((COLS, RANK), BF16),
            pltpu.VMEM((N, 8, 128), F32),
            pltpu.VMEM((N, 8, 128), F32),
            pltpu.VMEM((N, 8, 128), F32),
            dma((2, N)), dma((2, N)),
            dma((2, 2, 4, 2)), dma((2, 2, 4, 2)),
            dma((2, 2, 4, 2)), dma((2, 2, 4, 2)),
            dma((2, N)), dma((2, N)),
            dma((3, N)), dma((3, N)),
        ],
        compiler_params=pltpu.CompilerParams(
            collective_id=1, has_side_effects=True, vmem_limit_bytes=VMEM_LIMIT
        ),
    )(momentum, wide, low)


def body(momentum, right_prev):
    left_raw, gram, wide = first(momentum, right_prev)
    left_factor, low = whiten(left_raw, gram)
    new_momentum, right_factor = last(momentum, wide, low)
    return new_momentum, left_factor, right_factor


def solution(mesh):
    in_specs = (P("fsdp", "tensor"), P(("tensor", "fsdp"), None))
    out_specs = (P("fsdp", "tensor"), P("fsdp", None), P(("tensor", "fsdp"), None))
    return jax.shard_map(body, mesh=mesh, in_specs=in_specs, out_specs=out_specs, check_vma=False)
```

time: 677 us -> 152 us (0.22)
  the two profiles are of different devices: /device:TPU:1 before, /device:TPU:8 now
where the time goes in v1:
time: 152 us; the launch traced here: 151 us
  Pallas kernels  147 us (97%)
  local copies, waits for them, and re-layouts  3.57 us (2%)
    pallas_call x1, Pallas kernels, first(): pl.pallas_call(first_kernel, out_shape=(jax.ShapeDtypeStruct((ROWS, RANK)...  70.2 us
    pallas_call x1, Pallas kernels, last(): pl.pallas_call(last_kernel, out_shape=(jax.ShapeDtypeStruct((ROWS, COLS),...  65.4 us
    pallas_call x1, Pallas kernels, whiten(): pl.pallas_call(whiten_kernel, out_shape=(jax.ShapeDtypeStruct((ROWS, RANK...  11.5 us
    unnamed x4, local copies, waits for them, and re-layouts  3.57 us

profile of v1, /device:TPU:8, one launch (start us, length us, event | category | flops | bytes accessed | tf_op | source)
XLA Modules:
  0.0 151.3 jit_solution(2724720125243525469)
XLA Ops:
  0.6 70.2 %shard_map.49 = (f32[256,256]{1,0:T(8,128)}, f32[64,8,128]{2,1,0:T(8,128)}, bf16[4096,256]{1,0:T(8,128)(2,1)}) custom-call(bf16[256,3840]{1,0:T(8,128)(2,1)} %m_ref.3, bf16[60,256]{1,0:T(8,128)(2,1)} %r_ref.1), custom_call_target="tpu_custom_call" | custom-call | tf_op jit(solution)/shard_map/pallas_call | solution.py:257
  70.8 11.5 %shard_map.50 = (f32[256,256]{1,0:T(8,128)}, bf16[256,256]{1,0:T(8,128)(2,1)}) custom-call(f32[256,256]{1,0:T(8,128)} %get-tuple-element.11.left_ref, f32[64,8,128]{2,1,0:T(8,128)} %get-tuple-element.12.gram_ref), custom_call_target="tpu_custom_call" | custom-call | tf_op jit(solution)/shard_map/pallas_call | solution.py:361
  82.3 65.4 %shard_map.51 = (bf16[256,3840]{1,0:T(8,128)(2,1)}, bf16[60,256]{1,0:T(8,128)(2,1)}) custom-call(bf16[256,3840]{1,0:T(8,128)(2,1)} %m_ref.3, bf16[4096,256]{1,0:T(8,128)(2,1)} %get-tuple-element.10.wide_ref, bf16[256,256]{1,0:T(8,128)(2,1)} %get-tuple-element.13.low_ref), custom_call_target="tpu_custom_call" | custom-call | tf_op jit(solution)/shard_map/pallas_call | solution.py:509
  147.7 0.0 copy-start
  147.7 2.9 %copy.7 = bf16[256,3840]{1,0:T(8,128)(2,1)} copy(bf16[256,3840]{1,0:T(8,128)(2,1)} %get-tuple-element.20) | data formatting | bytes 3932160
  150.7 0.0 copy-done
  150.7 0.6 copy.8
Async XLA Ops:
  147.7 3.0 %copy-start = (bf16[60,256]{1,0:T(8,128)(2,1)S(1)}, bf16[60,256]{1,0:T(8,128)(2,1)}, u32[]{:S(2)}) copy-start(bf16[60,256]{1,0:T(8,128)(2,1)} %get-tuple-element.22) | copy-start | bytes 92164

commit v2 on v0

v2 whole, which is shorter than its diff:
```python
import math

import jax
import jax.numpy as jnp
from jax import lax
from jax.experimental import pallas as pl
from jax.experimental.pallas import tpu as pltpu
from jax.sharding import PartitionSpec as P

D = 16384
FF = 30720
RANK = 256
ROWS = 256
COLS = 3840
SHARE = 60
PAD = 64
N = 8
HALF = 128
MESH = pl.DeviceIdType.MESH
F32 = jnp.float32
BF16 = jnp.bfloat16
HIGHEST = lax.Precision.HIGHEST
VMEM_LIMIT = 40 * 1024 * 1024


def place():
    f, t = lax.axis_index("fsdp"), lax.axis_index("tensor")
    return lax.div(f, N), lax.rem(f, N), t


def up(i, d):
    return lax.rem(i + d, N)


def remote(src, dst, send, recv, z, y, t):
    return pltpu.make_async_remote_copy(
        src_ref=src,
        dst_ref=dst,
        send_sem=send,
        recv_sem=recv,
        device_id=(z * N + y, t),
        device_id_type=MESH,
    )


def greet(z, y, t):
    barrier = pltpu.get_barrier_semaphore()
    for d in range(1, N):
        for there in ((z, up(y, d), t), (up(z, d), y, t), (z, y, up(t, d))):
            pl.semaphore_signal(
                barrier, inc=1, device_id=(there[0] * N + there[1], there[2]), device_id_type=MESH
            )
    pl.semaphore_wait(barrier, 3 * (N - 1))


def exchange(axis, here, src_of, dst_of, send, recv):
    z, y, t = here
    me = here[axis]
    sent, waits = [], []
    for d in (4, 3, 5, 2, 6, 1, 7):
        peer = up(me, d)
        there = [z, y, t]
        there[axis] = peer
        copy = remote(src_of(peer), dst_of(me), send.at[d], recv.at[d], *there)
        copy.start()
        sent.append(copy)
        origin = up(me, N - d)
        waits.append(remote(src_of(peer), dst_of(origin), send.at[d], recv.at[d], *there))
    return sent, waits


def strip(buf, half, i, unit):
    if half == 0:
        return buf.at[0, i, pl.ds(4 * unit, 4)]
    return buf.at[1, pl.ds(4 * unit, 4), i]


def ring_peer(here, half, way):
    z, y, t = here
    step = 1 if way == 0 else N - 1
    return (up(z, step), y, t) if half == 0 else (z, up(y, step), t)


SLOTS = (0, 1, 7, 2, 6, 3, 5, 4)
WAVES = ((0, 1), (1, 3), (4, 4))


def gather(here, rel, arrive, after, one_send, one_recv, two_send, two_recv):
    z, y, t = here
    sent, first = [], {}
    for slot in range(1, N):
        for half in (0, 1):
            there = list(here)
            there[1 - half] = up(here[1 - half], SLOTS[slot])
            copy = remote(
                rel.at[half, here[half], 0], rel.at[half, here[half], slot],
                one_send.at[half, slot], one_recv.at[half, slot], *there,
            )
            copy.start()
            sent.append(copy)
            first[half, slot] = copy

    def piece(half, way, s, wave):
        me = here[half]
        i = up(me, N - s) if way == 0 else up(me, s)
        start, count = WAVES[wave]
        return i, rel.at[half, i, pl.ds(start, count)]

    def ring(half, way, s, wave, src):
        return remote(
            src, src, two_send.at[half, way, s, wave], two_recv.at[half, way, s, wave],
            *ring_peer(here, half, way),
        )

    def arrived(half, way, s, wave):
        i, dst = piece(half, way, s + 1, wave)
        ring(half, way, s, wave, dst).wait_recv()
        return half, i, *WAVES[wave]

    forwards = lambda way, s, wave: s < 3 or (wave < 2) == (way == 0)
    for diag in range(6):
        came = []
        for wave in range(3):
            s = diag - wave
            if not 0 <= s < 4:
                continue
            for half in (0, 1):
                if s == 0:
                    start, count = WAVES[wave]
                    for slot in range(max(start, 1), start + count):
                        first[half, slot].wait_recv()
                    came.append((half, here[half], start, count))
                for way in (0, 1):
                    if not forwards(way, s, wave):
                        continue
                    if s > 0:
                        came.append(arrived(half, way, s - 1, wave))
                    copy = ring(half, way, s, wave, piece(half, way, s, wave)[1])
                    copy.start()
                    sent.append(copy)
        for chunk in came:
            arrive(*chunk)
        after(diag)
    for s in (2, 3):
        for wave in range(3):
            for half in (0, 1):
                for way in (0, 1):
                    if forwards(way, 3, wave) == (s == 3):
                        arrive(*arrived(half, way, s, wave))
    return sent


def placer(here, rel, buf):
    z, y, _ = here

    def arrive(half, i, start, count):
        for slot in range(start, start + count):
            origin = up(here[1 - half], N - SLOTS[slot])
            if half == 0:
                buf[0, i, origin] = rel[0, i, slot]
            else:
                buf[1, origin, i] = rel[1, i, slot]

    return arrive


def spread(offset, transposed):
    shape = (HALF, 256) if transposed else (256, HALF)
    n = lax.broadcasted_iota(jnp.int32, shape, 0 if transposed else 1)
    k = lax.broadcasted_iota(jnp.int32, shape, 1 if transposed else 0)
    high = n >= PAD
    want = offset + n - jnp.where(high, PAD - SHARE, 0)
    inside = n - jnp.where(high, PAD, 0) < SHARE
    return jnp.where((k == want) & inside, 1.0, 0.0).astype(BF16)


def invert_cholesky(w, between):
    lane = lax.broadcasted_iota(jnp.int32, (8, 128), 1)
    sub = lax.broadcasted_iota(jnp.int32, (8, 128), 0)
    row_of = lambda v, k: jnp.broadcast_to(v[k:k + 1, :], (8, 128))
    depth = 32
    for p in range(RANK // depth):
        base = p * depth
        b0 = base // 128
        rows = [
            [w[base + 8 * a:base + 8 * a + 8, 128 * b:128 * b + 128] for b in (0, 1)]
            for a in range(depth // 8)
        ]
        for q in range(depth // 8):
            l0 = (base + 8 * q) % 128
            below = range(q, depth // 8)
            cols = {
                a: [
                    jnp.broadcast_to(rows[a][b0][:, l0 + k:l0 + k + 1], (8, 128))
                    for k in range(8)
                ]
                for a in below
            }
            for k in range(8):
                inv = lax.rsqrt(row_of(cols[q][k], k))
                here = lane == l0 + k
                fresh = [row_of(rows[q][b], k) for b in (0, 1)]
                fresh[b0] = jnp.where(here, 1.0, fresh[b0])
                fresh = [v * inv for v in fresh]
                scaled = {k2: row_of(cols[q][k2], k) * inv for k2 in range(k + 1, 8)}
                for a in below:
                    mult = cols[a][k] * inv
                    if a == q:
                        mult = jnp.where(sub > k, mult, 0.0)
                    for b in (0, 1):
                        old = rows[a][b]
                        if b == b0:
                            erase = here & (sub > k) if a == q else here
                            old = jnp.where(erase, 0.0, old)
                        new = old - mult * fresh[b]
                        if a == q:
                            new = jnp.where(sub == k, fresh[b], new)
                        rows[a][b] = new
                    for k2 in range(k + 1, 8):
                        cols[a][k2] = cols[a][k2] - mult * scaled[k2]
        panel = jnp.concatenate([jnp.concatenate(r, axis=1) for r in rows], axis=0)
        w[base:base + depth, :] = panel
        end = base + depth
        if end < RANK:
            first_row = end // 128 * 128
            at = lax.broadcasted_iota(jnp.int32, (depth, RANK), 1) - base
            over = (at > lax.broadcasted_iota(jnp.int32, (depth, RANK), 0)) & (at < depth)
            update = lax.dot_general(
                panel[:, first_row:], jnp.where(over, 0.0, panel), (((0,), (0,)), ((), ())),
                precision=HIGHEST, preferred_element_type=F32,
            )[end - first_row:, :]
            col = lax.broadcasted_iota(jnp.int32, (RANK - end, RANK), 1)
            old = jnp.where((col >= base) & (col < end), 0.0, w[end:, :])
            w[end:, :] = old - update
        between(p)


def sums_kernel(
    m_ref, r_ref, left_ref, low_ref, packed_ref, right_ref,
    rel, rel2, buf, buf2, mpad, wide, part, raw, got, gram, summed, tile_y, tile_z, w, terms, land, near, rest,
    sq_y, sq_z, sq_t,
    a_send, a_recv, b_send, b_recv, c_send, c_recv, d_send, d_recv,
    e_send, e_recv, f_send, f_recv, r_send, r_recv, s_send, s_recv,
):
    here = place()
    z, y, t = here
    n = lax.broadcasted_iota(jnp.int32, (PAD, SHARE), 0)
    k = lax.broadcasted_iota(jnp.int32, (PAD, SHARE), 1)
    longer = jnp.where(n == k, 1.0, 0.0).astype(BF16)
    for half in (0, 1):
        rel[half, here[half], 0] = jnp.dot(
            longer, r_ref[:, half * HALF:(half + 1) * HALF], preferred_element_type=F32
        ).astype(BF16)
    greet(z, y, t)
    def widen(diag):
        if diag > 3:
            return
        for i in range(8 * diag, 8 * diag + 8):
            start = min(120 * i // 128 * 128, COLS - 256)
            window = m_ref[:, start:start + 256]
            mpad[:, i * 128:(i + 1) * 128] = jnp.dot(
                window, spread(120 * i - start, False), preferred_element_type=F32
            ).astype(BF16)
            wide[i * 128:(i + 1) * 128, :] = lax.dot_general(
                spread(120 * i - start, True), window, (((1,), (1,)), ((), ())),
                preferred_element_type=F32,
            ).astype(BF16)

    sent = gather(here, rel, placer(here, rel, buf), widen, a_send, a_recv, b_send, b_recv)

    width = N * PAD
    for half in (0, 1):
        total = jnp.zeros((ROWS, HALF), F32)
        for i in range(N):
            total += jnp.dot(
                mpad[:, i * width:(i + 1) * width],
                buf[half, i].reshape(width, HALF),
                preferred_element_type=F32,
            )
        part[:, half * HALF:(half + 1) * HALF] = total

    rows = ROWS // N
    piece = lambda i: pl.ds(pl.multiple_of(i * rows, rows), rows)
    more, waits = exchange(
        2, here, lambda p: part.at[piece(p)], lambda i: got.at[i], c_send.at[0], c_recv.at[0]
    )
    sent += more
    got[t] = part[piece(t), :]
    for copy in waits:
        copy.wait_recv()
    own = got[0]
    for i in range(1, N):
        own += got[i]
    raw[piece(t), :] = own
    more, waits = exchange(
        2, here, lambda p: raw.at[piece(t)], lambda i: raw.at[piece(i)],
        c_send.at[1], c_recv.at[1],
    )
    sent += more
    for copy in waits:
        copy.wait_recv()

    rows_all = raw[...]
    product = lax.dot_general(
        rows_all, rows_all, (((0,), (0,)), ((), ())),
        precision=HIGHEST, preferred_element_type=F32,
    )
    for i in range(64):
        r, c = i // 2 * 8, i % 2 * 128
        gram[i] = product[r:r + 8, c:c + 128]
    own_tile = t * N + y
    more, gram_waits = exchange(
        1, here, lambda p: gram.at[t * N + p], lambda i: tile_y.at[i], c_send.at[2], c_recv.at[2]
    )
    sent += more
    tile_y[y] = gram[own_tile]

    high = rows_all.astype(BF16)
    rows_all = rows_all - high.astype(F32)
    middle = rows_all.astype(BF16)
    lowest = (rows_all - middle.astype(F32)).astype(BF16)
    for i in range(N):
        block = wide[i * width:(i + 1) * width, :]
        total = jnp.dot(block, lowest, preferred_element_type=F32)
        total += jnp.dot(block, middle, preferred_element_type=F32)
        total += jnp.dot(block, high, preferred_element_type=F32)
        for half in (0, 1):
            terms[half, i] = total[:, half * HALF:(half + 1) * HALF].reshape(N, PAD, HALF)

    def order(way):
        a, b = way, 1 - way
        return ((0, a), (1, b), (1, a), (2, b), (2, a), (3, b), (3, a))

    def ring_send(half, way, s, unit, src):
        copy = remote(
            src, land.at[half, way, s, unit],
            r_send.at[half, way, s, unit], r_recv.at[half, way, s, unit],
            *ring_peer(here, half, way),
        )
        copy.start()
        sent.append(copy)

    def own_term(half, way, s, unit):
        me = here[half]
        return strip(terms, half, up(me, 4 - s) if way == 0 else up(me, 4 + s), unit)

    def tick(k):
        for half in (0, 1):
            for way in (0, 1):
                s, unit = order(way)[k]
                slot = land.at[half, way, s, unit]
                remote(
                    slot, slot, r_send.at[half, way, s, unit], r_recv.at[half, way, s, unit],
                    *ring_peer(here, half, way),
                ).wait_recv()
                if s < 3:
                    slot[...] = slot[...] + own_term(half, way, s + 1, unit)[...]
                    ring_send(half, way, s + 1, unit, slot)
                elif k == 5:
                    mine = strip(terms, half, here[half], unit)
                    near[half, pl.ds(4 * unit, 4)] = mine[...] + slot[...]
                else:
                    near[half, pl.ds(4 * unit, 4)] = near[half, pl.ds(4 * unit, 4)] + slot[...]

    for k in (0, 1):
        for half in (0, 1):
            for way in (0, 1):
                s, unit = order(way)[k]
                ring_send(half, way, s, unit, own_term(half, way, s, unit))

    def added(tiles):
        total = tiles[0]
        for i in range(1, N):
            total += tiles[i]
        return total

    def finish(waits):
        for copy in waits:
            copy.wait_recv()

    finish(gram_waits)
    tile_z[z] = added(tile_y)
    more, gram_waits = exchange(
        0, here, lambda p: tile_z.at[z], lambda i: tile_z.at[i], c_send.at[3], c_recv.at[3]
    )
    sent += more
    tick(0)
    tick(1)
    finish(gram_waits)
    summed[own_tile] = added(tile_z)
    more, gram_waits = exchange(
        1, here, lambda p: summed.at[own_tile], lambda i: summed.at[t * N + i],
        c_send.at[4], c_recv.at[4],
    )
    sent += more
    tick(2)
    finish(gram_waits)
    block = lambda i: summed.at[pl.ds(pl.multiple_of(i * N, N), N)]
    more, gram_waits = exchange(
        2, here, lambda p: block(t), lambda i: block(i), c_send.at[5], c_recv.at[5]
    )
    sent += more
    tick(3)
    finish(gram_waits)

    for i in range(64):
        r, c = i // 2 * 8, i % 2 * 128
        w[r:r + 8, c:c + 128] = summed[i]
    share_waits = []

    def between(p):
        if p < 3:
            tick(4 + p)
        if p == 2:
            for half in (0, 1):
                more, waits = exchange(
                    1 - half, here, lambda q: near.at[half, q], lambda i: rest.at[half, i],
                    d_send.at[half], d_recv.at[half],
                )
                sent.extend(more)
                share_waits.extend(waits)
                rest[half, here[1 - half]] = near[half, here[1 - half]]

    invert_cholesky(w, between)
    row = lax.broadcasted_iota(jnp.int32, (RANK, RANK), 0)
    col = lax.broadcasted_iota(jnp.int32, (RANK, RANK), 1)
    w[...] = jnp.where(col <= row, w[...], 0.0)
    solve = lambda rows: lax.dot_general(
        rows, w[...], (((1,), (1,)), ((), ())), precision=HIGHEST, preferred_element_type=F32
    )
    finish(share_waits)
    right = solve(jnp.concatenate([added(rest.at[0]), added(rest.at[1])], axis=1))
    for half in (0, 1):
        rel2[half, here[half], 0] = right[:, half * HALF:(half + 1) * HALF].astype(BF16)
    squares = jnp.sum(right * right, axis=0, keepdims=True)
    sq_y[y] = jnp.concatenate(
        [squares[:, :HALF], squares[:, HALF:], jnp.zeros((6, HALF), F32)], axis=0
    )
    square_waits = []

    def square_step(axis, tiles):
        me = here[axis]
        more, waits = exchange(
            axis, here, lambda p: tiles.at[me], lambda i: tiles.at[i],
            s_send.at[axis], s_recv.at[axis],
        )
        sent.extend(more)
        square_waits[:] = waits

    def beside(diag):
        if diag == 0:
            square_step(1, sq_y)
            left = solve(raw[...])
            left_ref[...] = left
            low_ref[...] = left.astype(BF16)
        elif diag == 2:
            finish(square_waits)
            sq_z[z] = added(sq_y)
            square_step(0, sq_z)
        elif diag == 4:
            finish(square_waits)
            sq_t[t] = added(sq_z)
            square_step(2, sq_t)

    sent += gather(here, rel2, placer(here, rel2, buf2), beside, e_send, e_recv, f_send, f_recv)

    group = 4 * SHARE
    n = lax.broadcasted_iota(jnp.int32, (group, 256), 0)
    k = lax.broadcasted_iota(jnp.int32, (group, 256), 1)
    skip = sum(jnp.where(n >= SHARE * i, PAD - SHARE, 0) for i in (1, 2, 3))
    close = jnp.where(k == n + skip, 1.0, 0.0).astype(BF16)
    for g in range(16):
        for half in (0, 1):
            wider = buf2[half, g // 2, g % 2 * 4:g % 2 * 4 + 4].reshape(256, HALF)
            packed_ref[g * group:(g + 1) * group, half * HALF:(half + 1) * HALF] = jnp.dot(
                close, wider, preferred_element_type=F32
            ).astype(BF16)

    finish(square_waits)
    total = added(sq_t)
    scale = lax.rsqrt(total / FF + 1e-06)
    right = jnp.concatenate(
        [right[:, :HALF] * scale[0:1, :], right[:, HALF:] * scale[1:2, :]], axis=1
    )
    right_ref[...] = right[:SHARE, :].astype(BF16)
    for copy in sent:
        copy.wait_send()


def sums(momentum, right_prev):
    dma = pltpu.SemaphoreType.DMA
    return pl.pallas_call(
        sums_kernel,
        out_shape=(
            jax.ShapeDtypeStruct((ROWS, RANK), F32),
            jax.ShapeDtypeStruct((ROWS, RANK), BF16),
            jax.ShapeDtypeStruct((COLS, RANK), BF16),
            jax.ShapeDtypeStruct((SHARE, RANK), BF16),
        ),
        in_specs=[pl.BlockSpec(memory_space=pltpu.VMEM)] * 2,
        out_specs=[pl.BlockSpec(memory_space=pltpu.VMEM)] * 4,
        scratch_shapes=[
            pltpu.VMEM((2, N, N, PAD, HALF), BF16),
            pltpu.VMEM((2, N, N, PAD, HALF), BF16),
            pltpu.VMEM((2, N, N, PAD, HALF), BF16),
            pltpu.VMEM((2, N, N, PAD, HALF), BF16),
            pltpu.VMEM((ROWS, 64 * PAD), BF16),
            pltpu.VMEM((64 * PAD, ROWS), BF16),
            pltpu.VMEM((ROWS, RANK), F32),
            pltpu.VMEM((ROWS, RANK), F32),
            pltpu.VMEM((N, ROWS // N, RANK), F32),
            pltpu.VMEM((64, 8, 128), F32),
            pltpu.VMEM((64, 8, 128), F32),
            pltpu.VMEM((N, 8, 128), F32),
            pltpu.VMEM((N, 8, 128), F32),
            pltpu.VMEM((RANK, RANK), F32),
            pltpu.VMEM((2, N, N, PAD, HALF), F32),
            pltpu.VMEM((2, 2, 4, 2, 4, PAD, HALF), F32),
            pltpu.VMEM((2, N, PAD, HALF), F32),
            pltpu.VMEM((2, N, PAD, HALF), F32),
            pltpu.VMEM((N, 8, 128), F32),
            pltpu.VMEM((N, 8, 128), F32),
            pltpu.VMEM((N, 8, 128), F32),
            dma((2, N)), dma((2, N)),
            dma((2, 2, 4, 3)), dma((2, 2, 4, 3)),
            dma((6, N)), dma((6, N)),
            dma((2, N)), dma((2, N)),
            dma((2, N)), dma((2, N)),
            dma((2, 2, 4, 3)), dma((2, 2, 4, 3)),
            dma((2, 2, 4, 2)), dma((2, 2, 4, 2)),
            dma((3, N)), dma((3, N)),
        ],
        compiler_params=pltpu.CompilerParams(
            collective_id=0, has_side_effects=True, vmem_limit_bytes=VMEM_LIMIT
        ),
    )(momentum, right_prev)


STEP = 768


def correct_kernel(
    m_ref, left_ref, low_ref, packed_ref, share_ref, new_ref, factor_ref, right_ref, tile, sem
):
    copies = []
    for i in range(COLS // STEP):
        part = pl.ds(i * STEP, STEP)
        update = lax.dot_general(
            low_ref[...], packed_ref[part, :], (((1,), (1,)), ((), ())),
            preferred_element_type=F32,
        )
        tile[i] = (m_ref[:, part].astype(F32) - 0.5 * update).astype(BF16)
        copy = pltpu.make_async_copy(tile.at[i], new_ref.at[:, part], sem.at[i])
        copy.start()
        copies.append(copy)
    factor_ref[...] = math.sqrt(D) * left_ref[...]
    right_ref[...] = share_ref[...]
    for copy in copies:
        copy.wait()


def correct(momentum, left, low, packed, share):
    vmem = pl.BlockSpec(memory_space=pltpu.VMEM)
    return pl.pallas_call(
        correct_kernel,
        out_shape=(
            jax.ShapeDtypeStruct((ROWS, COLS), BF16),
            jax.ShapeDtypeStruct((ROWS, RANK), F32),
            jax.ShapeDtypeStruct((SHARE, RANK), BF16),
        ),
        in_specs=[vmem] * 5,
        out_specs=(pl.BlockSpec(memory_space=pl.ANY), vmem, vmem),
        scratch_shapes=[
            pltpu.VMEM((COLS // STEP, ROWS, STEP), BF16),
            pltpu.SemaphoreType.DMA((COLS // STEP,)),
        ],
        compiler_params=pltpu.CompilerParams(vmem_limit_bytes=12 * 1024 * 1024),
    )(momentum, left, low, packed, share)


def body(momentum, right_prev):
    left, low, packed, share = sums(momentum, right_prev)
    return correct(momentum, left, low, packed, share)


def solution(mesh):
    in_specs = (P("fsdp", "tensor"), P(("tensor", "fsdp"), None))
    out_specs = (P("fsdp", "tensor"), P("fsdp", None), P(("tensor", "fsdp"), None))
    return jax.shard_map(body, mesh=mesh, in_specs=in_specs, out_specs=out_specs, check_vma=False)
```

time: 677 us -> 132 us (0.19)
  the two profiles are of different devices: /device:TPU:1 before, /device:TPU:6 now
where the time goes in v2:
time: 132 us; the launch traced here: 131 us
  Pallas kernels  128 us (97%)
  local copies, waits for them, and re-layouts  2.3 us (2%)
    pallas_call x1, Pallas kernels, sums(): pl.pallas_call(sums_kernel, out_shape=(jax.ShapeDtypeStruct((ROWS, RANK),...  126 us

profile of v2, /device:TPU:6, one launch (start us, length us, event | category | flops | bytes accessed | tf_op | source)
XLA Modules:
  0.0 131.3 jit_solution(642660176371385446)
XLA Ops:
  0.6 0.0 copy-start
  0.6 1.5 %copy-done = bf16[256,3840]{1,0:T(8,128)(2,1)S(1)} copy-done((bf16[256,3840]{1,0:T(8,128)(2,1)S(1)}, bf16[256,3840]{1,0:T(8,128)(2,1)}, u32[]{:S(2)}) %copy-start) | copy-done | bytes 1966104
  2.2 0.0 copy-start.1
  2.2 0.8 copy-done.1
  2.9 125.8 %shard_map.49 = (f32[256,256]{1,0:T(8,128)S(1)}, bf16[256,256]{1,0:T(8,128)(2,1)S(1)}, bf16[3840,256]{1,0:T(8,128)(2,1)S(1)}, bf16[60,256]{1,0:T(8,128)(2,1)S(1)}) custom-call(bf16[256,3840]{1,0:T(8,128)(2,1)S(1)} %copy-done, bf16[60,256]{1,0:T(8,128)(2,1)S(1)} %copy-done.1), custom_call_target="tpu_custom_call" | custom-call | tf_op jit(solution)/shard_map/pallas_call | solution.py:492
  128.8 2.3 %shard_map.50 = (bf16[256,3840]{1,0:T(8,128)(2,1)}, f32[256,256]{1,0:T(8,128)}, bf16[60,256]{1,0:T(8,128)(2,1)}) custom-call(bf16[256,3840]{1,0:T(8,128)(2,1)S(1)} %copy-done, f32[256,256]{1,0:T(8,128)S(1)} %get-tuple-element.7.left_ref, bf16[256,256]{1,0:T(8,128)(2,1)S(1)} %get-tuple-element.8.low_ref, bf16[3840,256]{1,0:T(8,128)(2,1)S(1)} %get-tuple-element.9.packed_ref, ...), custom_call_target="tpu_custom_call" | custom-call | tf_op jit(solution)/shard_map/pallas_call | solution.py:564
Async XLA Ops:
  0.6 1.5 %copy-start = (bf16[256,3840]{1,0:T(8,128)(2,1)S(1)}, bf16[256,3840]{1,0:T(8,128)(2,1)}, u32[]{:S(2)}) copy-start(bf16[256,3840]{1,0:T(8,128)(2,1)} %m_ref.3) | copy-start | bytes 5898244
  2.2 0.8 copy-start.1

commit v3 on v2

v3 whole, which is shorter than its diff:
```python
import math

import jax
import jax.numpy as jnp
from jax import lax
from jax.experimental import pallas as pl
from jax.experimental.pallas import tpu as pltpu
from jax.sharding import PartitionSpec as P

D = 16384
FF = 30720
RANK = 256
ROWS = 256
COLS = 3840
SHARE = 60
PAD = 64
N = 8
HALF = 128
MESH = pl.DeviceIdType.MESH
F32 = jnp.float32
BF16 = jnp.bfloat16
HIGHEST = lax.Precision.HIGHEST
VMEM_LIMIT = 40 * 1024 * 1024


def place():
    f, t = lax.axis_index("fsdp"), lax.axis_index("tensor")
    return lax.div(f, N), lax.rem(f, N), t


def up(i, d):
    return lax.rem(i + d, N)


def remote(src, dst, send, recv, z, y, t):
    return pltpu.make_async_remote_copy(
        src_ref=src,
        dst_ref=dst,
        send_sem=send,
        recv_sem=recv,
        device_id=(z * N + y, t),
        device_id_type=MESH,
    )


def greet(z, y, t):
    barrier = pltpu.get_barrier_semaphore()
    for d in range(1, N):
        for there in ((z, up(y, d), t), (up(z, d), y, t), (z, y, up(t, d))):
            pl.semaphore_signal(
                barrier, inc=1, device_id=(there[0] * N + there[1], there[2]), device_id_type=MESH
            )
    pl.semaphore_wait(barrier, 3 * (N - 1))


def exchange(axis, here, src_of, dst_of, view, send, recv):
    me = here[axis]
    for d in (4, 3, 5, 2, 6, 1, 7):
        there = list(here)
        there[axis] = up(me, d)
        remote(src_of(there[axis]), dst_of(me), send, recv, *there).start()
    return remote(view, view, send, recv, *there)


def strip(buf, half, i, unit):
    if half == 0:
        return buf.at[0, i, pl.ds(4 * unit, 4)]
    return buf.at[1, pl.ds(4 * unit, 4), i]


STREAMS = [(unit, half, way) for unit in (0, 1) for half in (0, 1) for way in (0, 1)]


def ring_peer(here, half, way):
    z, y, t = here
    step = 1 if way == 0 else N - 1
    return (up(z, step), y, t) if half == 0 else (z, up(y, step), t)


def gather_first(here, buf, one_send, one_recv):
    waits = []
    for half in (0, 1):
        base = here[half] * N
        own = buf.at[half, base + here[1 - half]]
        waits.append(exchange(
            1 - half, here, lambda p: own, lambda i: buf.at[half, base + i],
            buf.at[half, pl.ds(0, N - 1)], one_send.at[half], one_recv.at[half],
        ))
    return waits


def gather_second(here, buf, one_send, two_recv, after):
    def ring(half, way, s, unit, i):
        part = buf.at[half, pl.ds(pl.multiple_of(i * N + 4 * unit, 4), 4)]
        return remote(
            part, part, one_send.at[half], two_recv.at[half, way, s, unit],
            *ring_peer(here, half, way),
        )

    def arrived(half, way, s, unit):
        me = here[half]
        i = up(me, N - 1 - s) if way == 0 else up(me, 1 + s)
        ring(half, way, s, unit, i).wait_recv()

    for s in range(4):
        for unit, half, way in STREAMS:
            if s == 3 and unit != way:
                continue
            if s > 0:
                arrived(half, way, s - 1, unit)
            me = here[half]
            ring(half, way, s, unit, up(me, N - s) if way == 0 else up(me, s)).start()
        after(s)
    for s in (2, 3):
        for unit, half, way in STREAMS:
            if (unit == way) == (s == 3):
                arrived(half, way, s, unit)


def gather_sent(here, buf, one_send, one_recv):
    for half in (0, 1):
        view = buf.at[half, pl.ds(0, N * N - 1)]
        remote(view, view, one_send.at[half], one_recv.at[half], *ring_peer(here, half, 0)).wait_send()


def chunks(buf, half, z, ys):
    if half == 0:
        return buf[0, z * N + ys[0]:z * N + ys[-1] + 1].reshape(len(ys) * PAD, HALF)
    return jnp.concatenate([buf[1, y * N + z] for y in ys], axis=0)


def spread(offset, transposed):
    shape = (HALF, 256) if transposed else (256, HALF)
    n = lax.broadcasted_iota(jnp.int32, shape, 0 if transposed else 1)
    k = lax.broadcasted_iota(jnp.int32, shape, 1 if transposed else 0)
    high = n >= PAD
    want = offset + n - jnp.where(high, PAD - SHARE, 0)
    inside = n - jnp.where(high, PAD, 0) < SHARE
    return jnp.where((k == want) & inside, 1.0, 0.0).astype(BF16)


def invert_cholesky(w, between):
    lane = lax.broadcasted_iota(jnp.int32, (8, 128), 1)
    sub = lax.broadcasted_iota(jnp.int32, (8, 128), 0)
    row_of = lambda v, k: jnp.broadcast_to(v[k:k + 1, :], (8, 128))
    depth = 32
    for p in range(RANK // depth):
        base = p * depth
        b0 = base // 128
        rows = [
            [w[base + 8 * a:base + 8 * a + 8, 128 * b:128 * b + 128] for b in (0, 1)]
            for a in range(depth // 8)
        ]
        for q in range(depth // 8):
            l0 = (base + 8 * q) % 128
            below = range(q, depth // 8)
            cols = {
                a: [
                    jnp.broadcast_to(rows[a][b0][:, l0 + k:l0 + k + 1], (8, 128))
                    for k in range(8)
                ]
                for a in below
            }
            for k in range(8):
                inv = lax.rsqrt(row_of(cols[q][k], k))
                here = lane == l0 + k
                fresh = [row_of(rows[q][b], k) for b in (0, 1)]
                fresh[b0] = jnp.where(here, 1.0, fresh[b0])
                fresh = [v * inv for v in fresh]
                scaled = {k2: row_of(cols[q][k2], k) * inv for k2 in range(k + 1, 8)}
                for a in below:
                    mult = cols[a][k] * inv
                    if a == q:
                        mult = jnp.where(sub > k, mult, 0.0)
                    for b in (0, 1):
                        old = rows[a][b]
                        if b == b0:
                            erase = here & (sub > k) if a == q else here
                            old = jnp.where(erase, 0.0, old)
                        new = old - mult * fresh[b]
                        if a == q:
                            new = jnp.where(sub == k, fresh[b], new)
                        rows[a][b] = new
                    for k2 in range(k + 1, 8):
                        cols[a][k2] = cols[a][k2] - mult * scaled[k2]
        panel = jnp.concatenate([jnp.concatenate(r, axis=1) for r in rows], axis=0)
        w[base:base + depth, :] = panel
        end = base + depth
        if end < RANK:
            first_row = end // 128 * 128
            at = lax.broadcasted_iota(jnp.int32, (depth, RANK), 1) - base
            over = (at > lax.broadcasted_iota(jnp.int32, (depth, RANK), 0)) & (at < depth)
            update = lax.dot_general(
                panel[:, first_row:], jnp.where(over, 0.0, panel), (((0,), (0,)), ((), ())),
                precision=HIGHEST, preferred_element_type=F32,
            )[end - first_row:, :]
            col = lax.broadcasted_iota(jnp.int32, (RANK - end, RANK), 1)
            old = jnp.where((col >= base) & (col < end), 0.0, w[end:, :])
            w[end:, :] = old - update
        between(p)


def sums_kernel(
    m_hbm, r_hbm, left_ref, low_ref, packed_ref, right_ref,
    m_ref, r_ref, buf, buf2, mpad, wide, part, raw, got, gram, summed, tile_y, tile_z, w, terms, land,
    near, rest, sq_t,
    load, a_send, a_recv, b_recv, c_send, c_recv, d_send, d_recv,
    e_send, e_recv, f_recv, r_send, r_recv,
):
    here = place()
    z, y, t = here
    load_r = pltpu.make_async_copy(r_hbm, r_ref, load.at[0])
    load_m = pltpu.make_async_copy(m_hbm, m_ref, load.at[1])
    load_r.start()
    load_m.start()
    greet(z, y, t)
    load_r.wait()
    n = lax.broadcasted_iota(jnp.int32, (PAD, SHARE), 0)
    k = lax.broadcasted_iota(jnp.int32, (PAD, SHARE), 1)
    longer = jnp.where(n == k, 1.0, 0.0).astype(BF16)
    own = jnp.dot(longer, r_ref[...], preferred_element_type=F32).astype(BF16)
    for half in (0, 1):
        buf[half, here[half] * N + here[1 - half]] = own[:, half * HALF:(half + 1) * HALF]
    waits = gather_first(here, buf, a_send, a_recv)

    load_m.wait()

    def widen(tiles, transposed):
        for i in tiles:
            start = min(120 * i // 128 * 128, COLS - 256)
            window = m_ref[:, start:start + 256]
            if transposed:
                wide[i * 128:(i + 1) * 128, :] = lax.dot_general(
                    spread(120 * i - start, True), window, (((1,), (1,)), ((), ())),
                    preferred_element_type=F32,
                ).astype(BF16)
            else:
                mpad[:, i * 128:(i + 1) * 128] = jnp.dot(
                    window, spread(120 * i - start, False), preferred_element_type=F32
                ).astype(BF16)

    widen(range(16), False)
    for wait in waits:
        wait.wait_recv()

    def beside(s):
        if s == 0:
            widen(range(16, 32), False)
        else:
            widen(range(11 * s - 11, min(11 * s, 32)), True)

    gather_second(here, buf, a_send, b_recv, beside)

    width = N * PAD
    total = jnp.zeros((ROWS, RANK), F32)
    for i in range(N):
        block = jnp.concatenate([chunks(buf, half, i, range(N)) for half in (0, 1)], axis=1)
        total += jnp.dot(
            mpad[:, i * width:(i + 1) * width], block, preferred_element_type=F32
        )
    part[...] = total

    def begin(axis, src_of, dst_of, view, k):
        return exchange(axis, here, src_of, dst_of, view, c_send.at[k], c_recv.at[k])

    def added(tiles):
        total = tiles[0]
        for i in range(1, N):
            total += tiles[i]
        return total

    rows = ROWS // N
    piece = lambda i: pl.ds(pl.multiple_of(i * rows, rows), rows)
    seven = pl.ds(0, N - 1)
    sent = [begin(2, lambda p: part.at[piece(p)], lambda i: got.at[i], got.at[seven], 0)]
    got[t] = part[piece(t), :]
    sent[-1].wait_recv()
    raw[piece(t), :] = added(got)
    sent.append(begin(
        2, lambda p: raw.at[piece(t)], lambda i: raw.at[piece(i)], raw.at[pl.ds(0, 7 * rows)], 1
    ))
    sent[-1].wait_recv()

    rows_all = raw[...]
    product = lax.dot_general(
        rows_all, rows_all, (((0,), (0,)), ((), ())),
        precision=HIGHEST, preferred_element_type=F32,
    )
    for i in range(64):
        r, c = i // 2 * 8, i % 2 * 128
        gram[i] = product[r:r + 8, c:c + 128]
    own_tile = t * N + y
    sent.append(begin(
        1, lambda p: gram.at[t * N + p], lambda i: tile_y.at[i], tile_y.at[seven], 2
    ))
    tile_y[y] = gram[own_tile]

    high = rows_all.astype(BF16)
    rows_all = rows_all - high.astype(F32)
    middle = rows_all.astype(BF16)
    lowest = (rows_all - middle.astype(F32)).astype(BF16)
    for i in range(N):
        block = wide[i * width:(i + 1) * width, :]
        total = jnp.dot(block, lowest, preferred_element_type=F32)
        total += jnp.dot(block, middle, preferred_element_type=F32)
        total += jnp.dot(block, high, preferred_element_type=F32)
        for half in (0, 1):
            terms[half, i] = total[:, half * HALF:(half + 1) * HALF].reshape(N, PAD, HALF)

    def order(way):
        a, b = way, 1 - way
        return ((0, a), (1, b), (1, a), (2, b), (2, a), (3, b), (3, a))

    def ring_copy(half, way, k, src):
        return remote(
            src, land.at[half, way * 7 + k], r_send, r_recv.at[half, way * 7 + k],
            *ring_peer(here, half, way),
        )

    def own_term(half, way, s, unit):
        me = here[half]
        return strip(terms, half, up(me, 4 - s) if way == 0 else up(me, 4 + s), unit)

    def tick(k):
        for half in (0, 1):
            for way in (0, 1):
                s, unit = order(way)[k]
                slot = land.at[half, way * 7 + k]
                ring_copy(half, way, k, slot).wait_recv()
                if s < 3:
                    slot[...] = slot[...] + own_term(half, way, s + 1, unit)[...]
                    ring_copy(half, way, k + 2, slot).start()
                elif k == 5:
                    mine = strip(terms, half, here[half], unit)
                    near[half, pl.ds(4 * unit, 4)] = mine[...] + slot[...]
                else:
                    near[half, pl.ds(4 * unit, 4)] = near[half, pl.ds(4 * unit, 4)] + slot[...]

    def ring_start(k):
        for half in (0, 1):
            for way in (0, 1):
                s, unit = order(way)[k]
                ring_copy(half, way, k, own_term(half, way, s, unit)).start()

    sent[-1].wait_recv()
    tile_z[z] = added(tile_y)
    sent.append(begin(
        0, lambda p: tile_z.at[z], lambda i: tile_z.at[i], tile_z.at[seven], 3
    ))
    ring_start(0)
    sent[-1].wait_recv()
    summed[own_tile] = added(tile_z)
    sent.append(begin(
        1, lambda p: summed.at[own_tile], lambda i: summed.at[t * N + i], summed.at[seven], 4
    ))
    ring_start(1)
    tick(0)
    sent[-1].wait_recv()
    block = lambda i: summed.at[pl.ds(pl.multiple_of(i * N, N), N)]
    sent.append(begin(
        2, lambda p: block(t), lambda i: block(i), summed.at[pl.ds(0, 7 * N)], 5
    ))
    tick(1)
    sent[-1].wait_recv()

    for i in range(64):
        r, c = i // 2 * 8, i % 2 * 128
        w[r:r + 8, c:c + 128] = summed[i]
    share_waits = []

    def between(p):
        if p < 5:
            tick(2 + p)
        if p == 4:
            for half in (0, 1):
                share_waits.append(exchange(
                    1 - half, here, lambda q: near.at[half, q], lambda i: rest.at[half, i],
                    rest.at[half, seven], d_send.at[half], d_recv.at[half],
                ))
                rest[half, here[1 - half]] = near[half, here[1 - half]]

    invert_cholesky(w, between)
    row = lax.broadcasted_iota(jnp.int32, (RANK, RANK), 0)
    col = lax.broadcasted_iota(jnp.int32, (RANK, RANK), 1)
    w[...] = jnp.where(col <= row, w[...], 0.0)
    solve = lambda rows: lax.dot_general(
        rows, w[...], (((1,), (1,)), ((), ())), precision=HIGHEST, preferred_element_type=F32
    )
    for wait in share_waits:
        wait.wait_recv()
    right = solve(jnp.concatenate([added(rest.at[0]), added(rest.at[1])], axis=1))

    squares = jnp.sum(right * right, axis=0, keepdims=True)
    row = lax.broadcasted_iota(jnp.int32, (PAD, RANK), 0)
    chunk = jnp.where(row < SHARE, right, 0.0)
    for i in range(3):
        piece_of = squares.astype(BF16).astype(F32)
        squares = squares - piece_of
        chunk = jnp.where(row == SHARE + i, piece_of, chunk)
    chunk = chunk.astype(BF16)
    for half in (0, 1):
        buf2[half, here[half] * N + here[1 - half]] = chunk[:, half * HALF:(half + 1) * HALF]
    waits = gather_first(here, buf2, e_send, e_recv)
    left = solve(raw[...])
    left_ref[...] = left
    low_ref[...] = left.astype(BF16)
    for wait in waits:
        wait.wait_recv()
    gather_second(here, buf2, e_send, f_recv, lambda s: None)

    sums_of = []
    for half in (0, 1):
        total = jnp.zeros((16, HALF), F32)
        for i in range(N * N):
            total += buf2[half, i, PAD - 16:, :].astype(F32)
        sums_of.append(total[12:13] + total[13:14] + total[14:15])
    sq_t[t] = jnp.concatenate(sums_of + [jnp.zeros((6, HALF), F32)], axis=0)
    sent.append(begin(2, lambda p: sq_t.at[t], lambda i: sq_t.at[i], sq_t.at[seven], 6))

    group = 4 * SHARE
    n = lax.broadcasted_iota(jnp.int32, (group, 256), 0)
    k = lax.broadcasted_iota(jnp.int32, (group, 256), 1)
    skip = sum(jnp.where(n >= SHARE * i, PAD - SHARE, 0) for i in (1, 2, 3))
    close = jnp.where(k == n + skip, 1.0, 0.0).astype(BF16)
    for g in range(16):
        ys = range(g % 2 * 4, g % 2 * 4 + 4)
        wider = jnp.concatenate([chunks(buf2, half, g // 2, ys) for half in (0, 1)], axis=1)
        packed_ref[g * group:(g + 1) * group, :] = jnp.dot(
            close, wider, preferred_element_type=F32
        ).astype(BF16)

    sent[-1].wait_recv()
    total = added(sq_t)
    scale = lax.rsqrt(total / FF + 1e-06)
    right = jnp.concatenate(
        [right[:, :HALF] * scale[0:1, :], right[:, HALF:] * scale[1:2, :]], axis=1
    )
    right_ref[...] = right[:SHARE, :].astype(BF16)
    for wait in sent + share_waits:
        wait.wait_send()
    gather_sent(here, buf, a_send, a_recv)
    gather_sent(here, buf2, e_send, e_recv)
    remote(land, land, r_send, r_recv.at[0, 0], *ring_peer(here, 0, 0)).wait_send()


def sums(momentum, right_prev):
    dma = pltpu.SemaphoreType.DMA
    return pl.pallas_call(
        sums_kernel,
        out_shape=(
            jax.ShapeDtypeStruct((ROWS, RANK), F32),
            jax.ShapeDtypeStruct((ROWS, RANK), BF16),
            jax.ShapeDtypeStruct((COLS, RANK), BF16),
            jax.ShapeDtypeStruct((SHARE, RANK), BF16),
        ),
        in_specs=[pl.BlockSpec(memory_space=pltpu.HBM)] * 2,
        out_specs=[pl.BlockSpec(memory_space=pltpu.VMEM)] * 4,
        scratch_shapes=[
            pltpu.VMEM((ROWS, COLS), BF16),
            pltpu.VMEM((SHARE, RANK), BF16),
            pltpu.VMEM((2, N * N, PAD, HALF), BF16),
            pltpu.VMEM((2, N * N, PAD, HALF), BF16),
            pltpu.VMEM((ROWS, 64 * PAD), BF16),
            pltpu.VMEM((64 * PAD, ROWS), BF16),
            pltpu.VMEM((ROWS, RANK), F32),
            pltpu.VMEM((ROWS, RANK), F32),
            pltpu.VMEM((N, ROWS // N, RANK), F32),
            pltpu.VMEM((64, 8, 128), F32),
            pltpu.VMEM((64, 8, 128), F32),
            pltpu.VMEM((N, 8, 128), F32),
            pltpu.VMEM((N, 8, 128), F32),
            pltpu.VMEM((RANK, RANK), F32),
            pltpu.VMEM((2, N, N, PAD, HALF), F32),
            pltpu.VMEM((2, 14, 4, PAD, HALF), F32),
            pltpu.VMEM((2, N, PAD, HALF), F32),
            pltpu.VMEM((2, N, PAD, HALF), F32),
            pltpu.VMEM((N, 8, 128), F32),
            dma((2,)),
            dma((2,)), dma((2,)), dma((2, 2, 4, 2)),
            dma((7,)), dma((7,)),
            dma((2,)), dma((2,)),
            dma((2,)), dma((2,)), dma((2, 2, 4, 2)),
            dma, dma((2, 14)),
        ],
        compiler_params=pltpu.CompilerParams(
            collective_id=0, has_side_effects=True, vmem_limit_bytes=VMEM_LIMIT
        ),
    )(momentum, right_prev)


STEP = 768


def correct_kernel(
    m_ref, left_ref, low_ref, packed_ref, share_ref, new_ref, factor_ref, right_ref, tile, sem
):
    copies = []
    for i in range(COLS // STEP):
        part = pl.ds(i * STEP, STEP)
        update = lax.dot_general(
            low_ref[...], packed_ref[part, :], (((1,), (1,)), ((), ())),
            preferred_element_type=F32,
        )
        tile[i] = (m_ref[:, part].astype(F32) - 0.5 * update).astype(BF16)
        copy = pltpu.make_async_copy(tile.at[i], new_ref.at[:, part], sem.at[i])
        copy.start()
        copies.append(copy)
    factor_ref[...] = math.sqrt(D) * left_ref[...]
    right_ref[...] = share_ref[...]
    for copy in copies:
        copy.wait()


def correct(momentum, left, low, packed, share):
    vmem = pl.BlockSpec(memory_space=pltpu.VMEM)
    return pl.pallas_call(
        correct_kernel,
        out_shape=(
            jax.ShapeDtypeStruct((ROWS, COLS), BF16),
            jax.ShapeDtypeStruct((ROWS, RANK), F32),
            jax.ShapeDtypeStruct((SHARE, RANK), BF16),
        ),
        in_specs=[vmem] * 5,
        out_specs=(pl.BlockSpec(memory_space=pl.ANY), vmem, vmem),
        scratch_shapes=[
            pltpu.VMEM((COLS // STEP, ROWS, STEP), BF16),
            pltpu.SemaphoreType.DMA((COLS // STEP,)),
        ],
        compiler_params=pltpu.CompilerParams(vmem_limit_bytes=12 * 1024 * 1024),
    )(momentum, left, low, packed, share)


def body(momentum, right_prev):
    left, low, packed, share = sums(momentum, right_prev)
    return correct(momentum, left, low, packed, share)


def solution(mesh):
    in_specs = (P("fsdp", "tensor"), P(("tensor", "fsdp"), None))
    out_specs = (P("fsdp", "tensor"), P("fsdp", None), P(("tensor", "fsdp"), None))
    return jax.shard_map(body, mesh=mesh, in_specs=in_specs, out_specs=out_specs, check_vma=False)
```

time: 132 us -> 124 us (0.939)
  the two profiles are of different devices: /device:TPU:6 before, /device:TPU:1 now
where the time goes in v3:
time: 124 us
  Pallas kernels  121 us (98%)
  local copies, waits for them, and re-layouts  2.3 us (2%)
    pallas_call x1, Pallas kernels, sums(): pl.pallas_call(sums_kernel, out_shape=(jax.ShapeDtypeStruct((ROWS, RANK),...  119 us

profile of v3, /device:TPU:1, one launch (start us, length us, event | category | flops | bytes accessed | tf_op | source)
XLA Modules:
  0.0 124.1 jit_solution(12082430434474105920)
XLA Ops:
  0.6 0.0 copy-start
  0.6 1.5 %copy-done = bf16[256,3840]{1,0:T(8,128)(2,1)S(1)} copy-done((bf16[256,3840]{1,0:T(8,128)(2,1)S(1)}, bf16[256,3840]{1,0:T(8,128)(2,1)}, u32[]{:S(2)}) %copy-start) | copy-done | bytes 1966104
  2.2 0.0 copy-start.1
  2.2 0.8 copy-done.1
  2.9 118.9 %shard_map.49 = (f32[256,256]{1,0:T(8,128)S(1)}, bf16[256,256]{1,0:T(8,128)(2,1)S(1)}, bf16[3840,256]{1,0:T(8,128)(2,1)S(1)}, bf16[60,256]{1,0:T(8,128)(2,1)S(1)}) custom-call(bf16[256,3840]{1,0:T(8,128)(2,1)S(1)} %copy-done, bf16[60,256]{1,0:T(8,128)(2,1)S(1)} %copy-done.1), custom_call_target="tpu_custom_call" | custom-call | tf_op jit(solution)/shard_map/pallas_call | solution.py:448
  121.8 2.3 %shard_map.50 = (bf16[256,3840]{1,0:T(8,128)(2,1)}, f32[256,256]{1,0:T(8,128)}, bf16[60,256]{1,0:T(8,128)(2,1)}) custom-call(bf16[256,3840]{1,0:T(8,128)(2,1)S(1)} %copy-done, f32[256,256]{1,0:T(8,128)S(1)} %get-tuple-element.7.left_ref, bf16[256,256]{1,0:T(8,128)(2,1)S(1)} %get-tuple-element.8.low_ref, bf16[3840,256]{1,0:T(8,128)(2,1)S(1)} %get-tuple-element.9.packed_ref, ...), custom_call_target="tpu_custom_call" | custom-call | tf_op jit(solution)/shard_map/pallas_call | solution.py:516
Async XLA Ops:
  0.6 1.5 %copy-start = (bf16[256,3840]{1,0:T(8,128)(2,1)S(1)}, bf16[256,3840]{1,0:T(8,128)(2,1)}, u32[]{:S(2)}) copy-start(bf16[256,3840]{1,0:T(8,128)(2,1)} %m_ref.1) | copy-start | bytes 5898244
  2.2 0.8 copy-start.1

commit v4 on v3

--- a/solution.py
+++ b/solution.py
@@ -50,7 +50,10 @@
             pl.semaphore_signal(
                 barrier, inc=1, device_id=(there[0] * N + there[1], there[2]), device_id_type=MESH
             )
-    pl.semaphore_wait(barrier, 3 * (N - 1))
+
+
+def greeted():
+    pl.semaphore_wait(pltpu.get_barrier_semaphore(), 3 * (N - 1))
 
 
 def exchange(axis, here, src_of, dst_of, view, send, recv):
@@ -221,6 +224,7 @@
     own = jnp.dot(longer, r_ref[...], preferred_element_type=F32).astype(BF16)
     for half in (0, 1):
         buf[half, here[half] * N + here[1 - half]] = own[:, half * HALF:(half + 1) * HALF]
+    greeted()
     waits = gather_first(here, buf, a_send, a_recv)
 
     load_m.wait()
@@ -342,25 +346,27 @@
                 s, unit = order(way)[k]
                 ring_copy(half, way, k, own_term(half, way, s, unit)).start()
 
+    ring_start(0)
+    ring_start(1)
     sent[-1].wait_recv()
     tile_z[z] = added(tile_y)
     sent.append(begin(
         0, lambda p: tile_z.at[z], lambda i: tile_z.at[i], tile_z.at[seven], 3
     ))
-    ring_start(0)
+    tick(0)
     sent[-1].wait_recv()
     summed[own_tile] = added(tile_z)
     sent.append(begin(
         1, lambda p: summed.at[own_tile], lambda i: summed.at[t * N + i], summed.at[seven], 4
     ))
-    ring_start(1)
-    tick(0)
+    tick(1)
     sent[-1].wait_recv()
     block = lambda i: summed.at[pl.ds(pl.multiple_of(i * N, N), N)]
     sent.append(begin(
         2, lambda p: block(t), lambda i: block(i), summed.at[pl.ds(0, 7 * N)], 5
     ))
-    tick(1)
+    tick(2)
+    tick(3)
     sent[-1].wait_recv()
 
     for i in range(64):
@@ -369,9 +375,9 @@
     share_waits = []
 
     def between(p):
-        if p < 5:
-            tick(2 + p)
-        if p == 4:
+        if p < 3:
+            tick(4 + p)
+        if p == 2:
             for half in (0, 1):
                 share_waits.append(exchange(
                     1 - half, here, lambda q: near.at[half, q], lambda i: rest.at[half, i],

time: 124 us -> 124 us (level)
  no operation moved by 1% of the time
where the time goes in v4:
time: 124 us
  Pallas kernels  121 us (98%)
  local copies, waits for them, and re-layouts  2.3 us (2%)
    pallas_call x1, Pallas kernels, sums(): pl.pallas_call(sums_kernel, out_shape=(jax.ShapeDtypeStruct((ROWS, RANK),...  118 us

profile of v4, /device:TPU:1, one launch (start us, length us, event | category | flops | bytes accessed | tf_op | source)
XLA Modules:
  0.0 123.7 jit_solution(6241872316721615931)
XLA Ops:
  0.6 0.0 copy-start
  0.6 1.5 %copy-done = bf16[256,3840]{1,0:T(8,128)(2,1)S(1)} copy-done((bf16[256,3840]{1,0:T(8,128)(2,1)S(1)}, bf16[256,3840]{1,0:T(8,128)(2,1)}, u32[]{:S(2)}) %copy-start) | copy-done | bytes 1966104
  2.2 0.0 copy-start.1
  2.2 0.8 copy-done.1
  2.9 118.4 %shard_map.49 = (f32[256,256]{1,0:T(8,128)S(1)}, bf16[256,256]{1,0:T(8,128)(2,1)S(1)}, bf16[3840,256]{1,0:T(8,128)(2,1)S(1)}, bf16[60,256]{1,0:T(8,128)(2,1)S(1)}) custom-call(bf16[256,3840]{1,0:T(8,128)(2,1)S(1)} %copy-done, bf16[60,256]{1,0:T(8,128)(2,1)S(1)} %copy-done.1), custom_call_target="tpu_custom_call" | custom-call | tf_op jit(solution)/shard_map/pallas_call | solution.py:454
  121.3 2.3 %shard_map.50 = (bf16[256,3840]{1,0:T(8,128)(2,1)}, f32[256,256]{1,0:T(8,128)}, bf16[60,256]{1,0:T(8,128)(2,1)}) custom-call(bf16[256,3840]{1,0:T(8,128)(2,1)S(1)} %copy-done, f32[256,256]{1,0:T(8,128)S(1)} %get-tuple-element.7.left_ref, bf16[256,256]{1,0:T(8,128)(2,1)S(1)} %get-tuple-element.8.low_ref, bf16[3840,256]{1,0:T(8,128)(2,1)S(1)} %get-tuple-element.9.packed_ref, ...), custom_call_target="tpu_custom_call" | custom-call | tf_op jit(solution)/shard_map/pallas_call | solution.py:522
Async XLA Ops:
  0.6 1.5 %copy-start = (bf16[256,3840]{1,0:T(8,128)(2,1)S(1)}, bf16[256,3840]{1,0:T(8,128)(2,1)}, u32[]{:S(2)}) copy-start(bf16[256,3840]{1,0:T(8,128)(2,1)} %m_ref.1) | copy-start | bytes 5898244
  2.2 0.8 copy-start.1

commit v5 on v4

--- a/solution.py
+++ b/solution.py
@@ -204,20 +204,17 @@
 
 
 def sums_kernel(
-    m_hbm, r_hbm, left_ref, low_ref, packed_ref, right_ref,
-    m_ref, r_ref, buf, buf2, mpad, wide, part, raw, got, gram, summed, tile_y, tile_z, w, terms, land,
+    m_hbm, r_ref, left_ref, low_ref, packed_ref, right_ref,
+    m_ref, buf, buf2, mpad, wide, part, raw, got, gram, summed, tile_y, tile_z, w, terms, land,
     near, rest, sq_t,
     load, a_send, a_recv, b_recv, c_send, c_recv, d_send, d_recv,
     e_send, e_recv, f_recv, r_send, r_recv,
 ):
     here = place()
     z, y, t = here
-    load_r = pltpu.make_async_copy(r_hbm, r_ref, load.at[0])
-    load_m = pltpu.make_async_copy(m_hbm, m_ref, load.at[1])
-    load_r.start()
+    load_m = pltpu.make_async_copy(m_hbm, m_ref, load)
     load_m.start()
     greet(z, y, t)
-    load_r.wait()
     n = lax.broadcasted_iota(jnp.int32, (PAD, SHARE), 0)
     k = lax.broadcasted_iota(jnp.int32, (PAD, SHARE), 1)
     longer = jnp.where(n == k, 1.0, 0.0).astype(BF16)
@@ -459,11 +456,10 @@
             jax.ShapeDtypeStruct((COLS, RANK), BF16),
             jax.ShapeDtypeStruct((SHARE, RANK), BF16),
         ),
-        in_specs=[pl.BlockSpec(memory_space=pltpu.HBM)] * 2,
+        in_specs=[pl.BlockSpec(memory_space=pltpu.HBM), pl.BlockSpec(memory_space=pltpu.VMEM)],
         out_specs=[pl.BlockSpec(memory_space=pltpu.VMEM)] * 4,
         scratch_shapes=[
             pltpu.VMEM((ROWS, COLS), BF16),
-            pltpu.VMEM((SHARE, RANK), BF16),
             pltpu.VMEM((2, N * N, PAD, HALF), BF16),
             pltpu.VMEM((2, N * N, PAD, HALF), BF16),
             pltpu.VMEM((ROWS, 64 * PAD), BF16),
@@ -481,7 +477,7 @@
             pltpu.VMEM((2, N, PAD, HALF), F32),
             pltpu.VMEM((2, N, PAD, HALF), F32),
             pltpu.VMEM((N, 8, 128), F32),
-            dma((2,)),
+            dma,
             dma((2,)), dma((2,)), dma((2, 2, 4, 2)),
             dma((7,)), dma((7,)),
             dma((2,)), dma((2,)),

time: 124 us -> 124 us (level)
  no operation moved by 1% of the time
where the time goes in v5:
time: 124 us
  Pallas kernels  121 us (98%)
  local copies, waits for them, and re-layouts  2.3 us (2%)
    pallas_call x1, Pallas kernels, sums(): pl.pallas_call(sums_kernel, out_shape=(jax.ShapeDtypeStruct((ROWS, RANK),...  118 us

profile of v5, /device:TPU:1, one launch (start us, length us, event | category | flops | bytes accessed | tf_op | source)
XLA Modules:
  0.0 123.5 jit_solution(13498730134829829950)
XLA Ops:
  0.6 0.0 copy-start
  0.6 1.5 %copy-done = bf16[256,3840]{1,0:T(8,128)(2,1)S(1)} copy-done((bf16[256,3840]{1,0:T(8,128)(2,1)S(1)}, bf16[256,3840]{1,0:T(8,128)(2,1)}, u32[]{:S(2)}) %copy-start) | copy-done | bytes 1966104
  2.2 0.0 copy-start.1
  2.2 0.8 copy-done.1
  2.9 118.3 %shard_map.49 = (f32[256,256]{1,0:T(8,128)S(1)}, bf16[256,256]{1,0:T(8,128)(2,1)S(1)}, bf16[3840,256]{1,0:T(8,128)(2,1)S(1)}, bf16[60,256]{1,0:T(8,128)(2,1)S(1)}) custom-call(bf16[256,3840]{1,0:T(8,128)(2,1)S(1)} %copy-done, bf16[60,256]{1,0:T(8,128)(2,1)S(1)} %copy-done.1), custom_call_target="tpu_custom_call" | custom-call | tf_op jit(solution)/shard_map/pallas_call | solution.py:451
  121.2 2.3 %shard_map.50 = (bf16[256,3840]{1,0:T(8,128)(2,1)}, f32[256,256]{1,0:T(8,128)}, bf16[60,256]{1,0:T(8,128)(2,1)}) custom-call(bf16[256,3840]{1,0:T(8,128)(2,1)S(1)} %copy-done, f32[256,256]{1,0:T(8,128)S(1)} %get-tuple-element.7.left_ref, bf16[256,256]{1,0:T(8,128)(2,1)S(1)} %get-tuple-element.8.low_ref, bf16[3840,256]{1,0:T(8,128)(2,1)S(1)} %get-tuple-element.9.packed_ref, ...), custom_call_target="tpu_custom_call" | custom-call | tf_op jit(solution)/shard_map/pallas_call | solution.py:518
Async XLA Ops:
  0.6 1.5 %copy-start = (bf16[256,3840]{1,0:T(8,128)(2,1)S(1)}, bf16[256,3840]{1,0:T(8,128)(2,1)}, u32[]{:S(2)}) copy-start(bf16[256,3840]{1,0:T(8,128)(2,1)} %m_ref.1) | copy-start | bytes 5898244
  2.2 0.8 copy-start.1
